TPU v7x, 128 devices: a whole 4x4x4 slice. The times are simulated.
128 devices in a mesh: patch: 128 (over z, x, y, core).
Axes of the slice: x: 4, y: 4, z: 4, core: 2. Of those that a mesh axis runs over, the one named last changes fastest.
Arguments:
- fine_nodes: float32 [32768, 512], P('patch'), may hold values from -6 to 6
- coarse_nodes: float32 [642, 512], replicated, may hold values from -6 to 6
- edge_feats: float32 [131072, 512], P('patch'), may hold values from -6 to 6
- senders: int32 [131072], P('patch'), may hold values from 0 to 1921, as said below
- receivers: int32 [131072], P('patch'), may hold values from 0 to 897, as said below
- send_rows: int32 [128, 128, 8], P('patch'), may hold values from 0 to 255
- w_edge_in: float32 [1536, 512], replicated, may hold values from -0.15625 to 0.15625
- w_edge_out: float32 [512, 512], replicated, may hold values from -0.25 to 0.25
- w_node_in: float32 [1024, 512], replicated, may hold values from -0.1875 to 0.1875
- w_node_out: float32 [512, 512], replicated, may hold values from -0.25 to 0.25
- cot_fine: float32 [32768, 512], P('patch'), may hold values from -6 to 6
- cot_coarse: float32 [642, 512], replicated, may hold values from -6 to 6
- cot_edges: float32 [131072, 512], P('patch'), may hold values from -6 to 6
Outputs:
- grad_fine: float32 [32768, 512], P('patch')
- grad_coarse: float32 [642, 512], replicated
- grad_edges: float32 [131072, 512], P('patch')
- grad_edge_in: float32 [1536, 512], replicated
- grad_edge_out: float32 [512, 512], replicated
- grad_node_in: float32 [1024, 512], replicated
- grad_node_out: float32 [512, 512], replicated
Inputs may be any that keep to these rules, and one draw needn't show every extreme that they name: Each patch's senders index its node table: its 256 fine nodes, then the 642 coarse nodes, then 8 halo rows from each patch in patch order; halo rows may come from any patch. Each patch's receivers index its own fine nodes, then the coarse nodes.
All inputs are finite; a program needn't handle non-finite values.
Results may differ from a plain program's by a relative error of at most 0.000076.
Values sent between devices are 32-bit elements; how exact they have to be, the bound alone decides.
A program may use at most 192 MiB of HBM per device.

v0:
```python
import math

import jax
import jax.numpy as jnp
from jax import lax
from jax.sharding import PartitionSpec as P


def mat_mul(left, right):
    return jnp.dot(left, right, precision=lax.Precision.HIGHEST, preferred_element_type=jnp.float32)


def layer_norm(values):
    center = values - jnp.mean(values, axis=1, keepdims=True)
    return center * lax.rsqrt(jnp.mean(center * center, axis=1, keepdims=True) + 1e-05)


def edge_tail(pre_act, edge_in, w_out):
    return edge_in + layer_norm(mat_mul(jax.nn.silu(pre_act), w_out))


def node_update(node_feats, aggregate, w_in, w_out):
    hidden = jax.nn.silu(mat_mul(jnp.concatenate([node_feats, aggregate], axis=1), w_in))
    return node_feats + layer_norm(mat_mul(hidden, w_out))


def per_device(
    fine_nodes,
    coarse_nodes,
    edge_feats,
    senders,
    receivers,
    send_rows,
    w_edge_in,
    w_edge_out,
    w_node_in,
    w_node_out,
    cot_fine,
    cot_coarse,
    cot_edges,
):
    fine_rows, feat_dim = fine_nodes.shape
    coarse_rows = coarse_nodes.shape[0]
    near_rows = fine_rows + coarse_rows
    peer_count = lax.axis_size("patch")
    slot_rows = send_rows.shape[2]
    send_list = send_rows[0].reshape(-1)
    outgoing = fine_nodes[send_list].reshape(peer_count, slot_rows, feat_dim)
    incoming = lax.all_to_all(outgoing, "patch", split_axis=0, concat_axis=0, tiled=True)
    near_table = jnp.concatenate([fine_nodes, coarse_nodes], axis=0)
    node_table = jnp.concatenate([near_table, incoming.reshape(-1, feat_dim)], axis=0)
    sent_feats = node_table[senders]
    recv_feats = near_table[receivers]
    stacked = jnp.concatenate([edge_feats, sent_feats, recv_feats], axis=1)
    pre_act = mat_mul(stacked, w_edge_in)
    new_edges, tail_back = jax.vjp(edge_tail, pre_act, edge_feats, w_edge_out)
    aggregate = jax.ops.segment_sum(new_edges, receivers, num_segments=near_rows)
    _, fine_back = jax.vjp(node_update, fine_nodes, aggregate[:fine_rows], w_node_in, w_node_out)
    grad_fine_own, grad_agg_fine, grad_in_fine, grad_out_fine = fine_back(cot_fine)
    coarse_part = aggregate[fine_rows:]
    coarse_agg = lax.psum(coarse_part, "patch")
    _, coarse_back = jax.vjp(node_update, coarse_nodes, coarse_agg, w_node_in, w_node_out)
    grad_coarse_direct, grad_agg_coarse, grad_in_coarse, grad_out_coarse = coarse_back(cot_coarse)
    grad_agg = jnp.concatenate([grad_agg_fine, grad_agg_coarse], axis=0)
    grad_new_edges = cot_edges + grad_agg[receivers]
    grad_pre, grad_edges_tail, edge_out_part = tail_back(grad_new_edges)
    grad_stacked = mat_mul(grad_pre, w_edge_in.T)
    grad_edges_in = grad_stacked[:, :feat_dim]
    grad_sent = grad_stacked[:, feat_dim : 2 * feat_dim]
    grad_recv = grad_stacked[:, 2 * feat_dim :]
    edge_in_part = mat_mul(stacked.T, grad_pre)
    grad_table = jax.ops.segment_sum(grad_sent, senders, num_segments=node_table.shape[0])
    grad_near = grad_table[:near_rows] + jax.ops.segment_sum(
        grad_recv, receivers, num_segments=near_rows
    )
    grad_halo = grad_table[near_rows:].reshape(peer_count, slot_rows, feat_dim)
    returned = lax.all_to_all(grad_halo, "patch", split_axis=0, concat_axis=0, tiled=True)
    grad_fine = (
        grad_fine_own
        + grad_near[:fine_rows]
        + jax.ops.segment_sum(returned.reshape(-1, feat_dim), send_list, num_segments=fine_rows)
    )
    grad_edges = grad_edges_tail + grad_edges_in
    coarse_grad_part = grad_near[fine_rows:]
    grad_coarse = grad_coarse_direct + lax.psum(coarse_grad_part, "patch")
    summed = lax.psum((edge_in_part, edge_out_part, grad_in_fine, grad_out_fine), "patch")
    node_in_total = summed[2] + grad_in_coarse
    node_out_total = summed[3] + grad_out_coarse
    edge_scale = 1.0 / math.sqrt(edge_feats.shape[0] * peer_count)
    node_scale = 1.0 / math.sqrt(fine_rows * peer_count + coarse_rows)
    return (
        grad_fine,
        grad_coarse,
        grad_edges,
        summed[0] * edge_scale,
        summed[1] * edge_scale,
        node_in_total * node_scale,
        node_out_total * node_scale,
    )


def solution(mesh):
    return jax.shard_map(
        per_device,
        mesh=mesh,
        in_specs=(
            P("patch", None),
            P(),
            P("patch", None),
            P("patch"),
            P("patch"),
            P("patch", None, None),
            P(),
            P(),
            P(),
            P(),
            P("patch", None),
            P(),
            P("patch", None),
        ),
        out_specs=(P("patch", None), P(), P("patch", None), P(), P(), P(), P()),
        check_vma=False,
    )
```

profile of v0, /device:TPU:1, one launch (start us, length us, event | category | flops | bytes accessed | tf_op | source)
XLA Modules:
  0.0 583.5 jit_solution(1184691562817358424)
XLA Ops:
  8.9 6.3 %gather_fusion = f32[1024,512]{1,0:T(8,128)} fusion(f32[256,512]{1,0:T(8,128)} %param.13, s32[1024]{0:T(1024)S(1)} %get-tuple-element.49), kind=kCustom, calls=%fused_computation | custom fusion | bytes 4198400 | tf_op jit(solution)/shard_map/gather | solution.py:48
  15.2 12.0 %all-to-all-start = ((f32[128,8,512]{2,1,0:T(8,128)}), f32[128,8,512]{2,1,0:T(8,128)}, u32[]{:S(2)}, u32[]{:S(2)}) async-start(f32[128,8,512]{2,1,0:T(8,128)} %bitcast.32), calls=%async_computation | async-start | bytes 4194304 | tf_op jit(solution)/shard_map/all_to_all | solution.py:49
  27.2 2.9 copy.28
  30.1 2.9 copy.26
  33.0 2.9 pad_maximum_fusion
  35.9 6.8 %gather_fusion.2 = f32[1024,512]{1,0:T(8,128)} fusion(f32[898,512]{1,0:T(8,128)} %pad_maximum_fusion, s32[1024]{0:T(1024)S(1)} %get-tuple-element.48), kind=kCustom, calls=%fused_computation.2 | custom fusion | bytes 4198400 | tf_op jit(solution)/shard_map/gather | solution.py:53
  42.6 2.7 constant_dynamic-update-slice_fusion.4
  46.9 10.5 %all-to-all-done = f32[128,8,512]{2,1,0:T(8,128)} async-done(((f32[128,8,512]{2,1,0:T(8,128)}), f32[128,8,512]{2,1,0:T(8,128)}, u32[]{:S(2)}, u32[]{:S(2)}) %all-to-all-start) | async-done | bytes 2097184 | tf_op jit(solution)/shard_map/all_to_all | solution.py:49
  57.4 12.5 %concatenate.19 = f32[1922,512]{1,0:T(8,128)} concatenate(f32[256,512]{1,0:T(8,128)} %param.13, f32[642,512]{1,0:T(8,128)} %param.14, f32[1024,512]{1,0:T(8,128)} %bitcast.2), dimensions={0} | concatenate | bytes 7872512 | tf_op jit(solution)/shard_map/concatenate | solution.py:51
  69.9 7.4 %gather_fusion.1 = f32[1024,512]{1,0:T(8,128)} fusion(f32[1922,512]{1,0:T(8,128)} %concatenate.19, s32[1024]{0:T(1024)S(1)} %fusion.54), kind=kCustom, calls=%fused_computation.1 | custom fusion | bytes 4198400 | tf_op jit(solution)/shard_map/gather | solution.py:52
  77.2 3.4 constant_dynamic-update-slice_fusion.1
  82.2 12.3 %fusion.73 = f32[1024,512]{1,0:T(8,128)S(1)} fusion(f32[1024,1536]{1,0:T(8,128)} %constant_dynamic-update-slice_fusion, f32[1536,512]{1,0:T(8,128)S(1)} %copy-done), kind=kOutput, calls=%fused_computation.117 | convolution fusion | flops 9663676416 | bytes 11534336 | tf_op jit(solution)/shard_map/dot_general | solution.py:10
  94.5 3.9 fusion.70
  102.7 2.9 copy.27
  105.6 19.4 %scatter_custom_fusion = f32[898,512]{1,0:T(8,128)} fusion(s32[1024]{0:T(1024)} %param.17, f32[1024,512]{1,0:T(8,128)} %copy.27, f32[]{:T(128)} %constant.15.clone.1), kind=kCustom, calls=%fused_computation.51 | custom fusion | flops 524288 | bytes 1839616 | tf_op jit(solution)/shard_map/scatter-add | solution.py:57
  126.9 2.5 slice.45
  129.4 3.9 fusion.31
  140.2 2.2 fusion.37
  142.4 3.1 fusion.30
  145.6 127.2 %all-reduce.4.cloned.1.call-done = f32[642,512]{1,0:T(8,128)} async-done(((f32[642,512]{1,0:T(8,128)}), f32[642,512]{1,0:T(8,128)}) %all-reduce.4.cloned.1.call-update) | async-done | bytes 1314832 | tf_op jit(solution)/shard_map/psum | solution.py:61
  272.8 2.7 constant_dynamic-update-slice_fusion.3
  275.5 6.6 %fusion.75 = f32[642,512]{1,0:T(8,128)S(1)} fusion(f32[642,1024]{1,0:T(8,128)} %constant_dynamic-update-slice_fusion.3, f32[1024,512]{1,0:T(8,128)S(1)} %copy-done.3), kind=kOutput, calls=%fused_computation.119 | convolution fusion | flops 4039114752 | bytes 6041600 | tf_op jit(solution)/shard_map/jvp()/dot_general | solution.py:10
  282.1 2.6 fusion.71
  285.8 2.7 fusion.18
  288.6 4.6 fusion.76
  297.1 6.8 %gather_fusion.3 = f32[1024,512]{1,0:T(8,128)} fusion(f32[898,512]{1,0:T(8,128)} %pad_maximum_fusion.1, s32[1024]{0:T(1024)S(1)} %get-tuple-element.48), kind=kCustom, calls=%fused_computation.3 | custom fusion | bytes 4198400 | tf_op jit(solution)/shard_map/gather | solution.py:65
  304.0 3.1 copy.29
  307.1 3.7 multiply_reduce_fusion
  313.2 7.9 %fusion.10 = f32[512,512]{1,0:T(8,128)} fusion(f32[1024,512]{0,1:T(8,128)S(1)} %get-tuple-element.31, f32[1024]{0:T(1024)S(1)} %negate_multiply_fusion, f32[1024,512]{1,0:T(8,128)S(1)} %copy-done.33), kind=kOutput, calls=%fused_computation.28 | convolution fusion | flops 3223846912 | bytes 5246976 | tf_op jit(solution)/shard_map/transpose(jvp())/dot_general | solution.py:10
  321.1 7.3 %fusion.1 = f32[1024,512]{1,0:T(8,128)S(1)} fusion(f32[1024,512]{1,0:T(8,128)S(1)} %copy-done.33, f32[512,512]{1,0:T(8,128)S(1)} %copy-done.31, f32[1024,512]{0,1:T(8,128)S(1)} %get-tuple-element.31, f32[1024]{0:T(1024)S(1)} %negate_multiply_fusion), kind=kOutput, calls=%fused_computation.11 | convolution fusion | flops 3226468352 | bytes 7344128 | tf_op jit(solution)/shard_map/transpose(jvp())/dot_general | solution.py:10
  328.4 12.1 %fusion.78 = f32[1536,512]{1,0:T(8,128)} fusion(f32[1024,1536]{1,0:T(8,128)S(1)} %bitcast.31, f32[1024,512]{1,0:T(8,128)S(1)} %fusion.1), kind=kOutput, calls=%fused_computation.122 | convolution fusion | flops 9663676416 | bytes 11534336 | tf_op jit(solution)/shard_map/dot_general | solution.py:10
  340.6 12.2 %fusion.77 = f32[1024,1536]{1,0:T(8,128)} fusion(f32[1024,512]{1,0:T(8,128)S(1)} %fusion.1, f32[1536,512]{1,0:T(8,128)S(1)} %copy-done), kind=kOutput, calls=%fused_computation.121 | convolution fusion | flops 9663676416 | bytes 11534336 | tf_op jit(solution)/shard_map/dot_general | solution.py:10
  352.7 9.5 %scatter_custom_fusion.1 = f32[1922,512]{1,0:T(8,128)} fusion(s32[1024]{0:T(1024)S(1)} %copy-done.27, f32[1024,1536]{1,0:T(8,128)} %fusion.77, f32[]{:T(128)} %constant.15.clone.1), kind=kCustom, calls=%fused_computation.15 | custom fusion | flops 524288 | bytes 6033920 | tf_op jit(solution)/shard_map/scatter-add | solution.py:72
  362.2 3.0 slice.47
  365.2 10.2 %scatter_custom_fusion.2 = f32[898,512]{1,0:T(8,128)} fusion(f32[898,512]{1,0:T(8,128)} %slice.47, s32[1024]{0:T(1024)} %param.17, f32[1024,1536]{1,0:T(8,128)} %fusion.77), kind=kCustom, calls=%fused_computation.13 | custom fusion | flops 524288 | bytes 3936256 | tf_op jit(solution)/shard_map/scatter-add | solution.py:73
  375.4 2.5 slice.51
  377.9 3.2 slice_bitcast_fusion
  381.1 7.1 %all-to-all-start.1 = ((f32[128,8,512]{2,1,0:T(8,128)}), f32[128,8,512]{2,1,0:T(8,128)}, u32[]{:S(2)}, u32[]{:S(2)}) async-start(f32[128,8,512]{2,1,0:T(8,128)} %slice_bitcast_fusion), calls=%async_computation.1 | async-start | bytes 4194304 | tf_op jit(solution)/shard_map/all_to_all | solution.py:77
  388.2 3.2 slice.52
  391.4 2.9 copy.33
  394.3 4.2 add.137
  398.5 2.9 copy.32
  401.4 2.3 slice_add_fusion.1
  403.7 19.7 %all-to-all-done.1 = f32[128,8,512]{2,1,0:T(8,128)} async-done(((f32[128,8,512]{2,1,0:T(8,128)}), f32[128,8,512]{2,1,0:T(8,128)}, u32[]{:S(2)}, u32[]{:S(2)}) %all-to-all-start.1) | async-done | bytes 2097184 | tf_op jit(solution)/shard_map/all_to_all | solution.py:77
  423.5 9.2 %scatter_custom_fusion.3 = f32[256,512]{1,0:T(8,128)} fusion(f32[256,512]{1,0:T(8,128)} %slice_add_fusion.1, s32[1024]{0:T(1024)S(1)} %reshape.188, f32[128,8,512]{2,1,0:T(8,128)} %all-to-all-done.1), kind=kCustom, calls=%fused_computation.17 | custom fusion | flops 524288 | bytes 2621440 | tf_op jit(solution)/shard_map/scatter-add | solution.py:81
  432.7 125.8 %all-reduce.6.cloned.1.call-done = (f32[642,512]{1,0:T(8,128)}, f32[1536,512]{1,0:T(8,128)}, f32[512,512]{1,0:T(8,128)}, f32[1024,512]{1,0:T(8,128)}, f32[512,512]{1,0:T(8,128)}) async-done(((f32[642,512]{1,0:T(8,128)}, f32[1536,512]{1,0:T(8,128)}, f32[512,512]{1,0:T(8,128)}, f32[1024,512]{1,0:T(8,128)}, f32[512,512]{1,0:T(8,128)}), (f32[642,512]{1,0:T(8,128)}, f32[1536,512]{1,0:T(8,128)}, ...) | async-done | bytes 8654864 | tf_op jit(solution)/shard_map/psum | solution.py:85
  558.5 6.3 %fusion.16 = f32[512,512]{1,0:T(8,128)} fusion(f32[512,512]{1,0:T(8,128)} %get-tuple-element.29, f32[642,512]{1,0:T(8,128)} %copy-done.24, f32[642]{0:T(1024)S(1)} %negate_multiply_fusion.1, f32[642,512]{1,0:T(8,128)} %copy-done.23), kind=kOutput, calls=%fused_computation.36 | convolution fusion | flops 2021725184 | bytes 4729352 | tf_op jit(solution)/shard_map/transpose(jvp())/dot_general | solution.py:10
  564.8 6.7 %add_multiply_fusion = f32[1024,512]{1,0:T(8,128)} fusion(f32[1024,512]{1,0:T(8,128)S(1)} %copy-done.22, f32[642,1024]{1,0:T(8,128)S(1)} %copy-done.7, f32[642,512]{1,0:T(8,128)S(1)} %copy-done.16), kind=kOutput, calls=%fused_computation.19 | convolution fusion | flops 4040163328 | bytes 8138752 | tf_op jit(solution)/shard_map/transpose(jvp())/dot_general | solution.py:10
  (112 shorter events, 30.3 us)
Async XLA Ops:
  7.2 75.0 %copy-start = (f32[1536,512]{1,0:T(8,128)S(1)}, f32[1536,512]{1,0:T(8,128)}, u32[]{:S(2)}) copy-start(f32[1536,512]{1,0:T(8,128)} %param.19) | copy-start | bytes 9437188
  15.2 42.1 %all-to-all-start = ((f32[128,8,512]{2,1,0:T(8,128)}), f32[128,8,512]{2,1,0:T(8,128)}, u32[]{:S(2)}, u32[]{:S(2)}) async-start(f32[128,8,512]{2,1,0:T(8,128)} %bitcast.32), calls=%async_computation | async-start | bytes 4194304 | tf_op jit(solution)/shard_map/all_to_all | solution.py:49
  27.2 245.6 %all-reduce.4.cloned.1.call-start = ((), (), s32[]{:S(2)}) async-start(), calls=%async_computation.2 | async-start | bytes 2654208 | tf_op jit(solution)/shard_map/psum | solution.py:61
  42.6 2.7 copy-start.13
  45.3 1.6 copy-start.27
  77.2 3.4 copy-start.12
  82.2 12.3 %copy-start.30 = (f32[512,512]{1,0:T(8,128)S(1)}, f32[512,512]{1,0:T(8,128)}, u32[]{:S(2)}) copy-start(f32[512,512]{1,0:T(8,128)} %param.20) | copy-start | bytes 3145732
  94.5 3.9 copy-start.32
  98.5 1.3 copy-start.4
  98.5 2.3 copy-start.14
  129.4 429.1 %all-reduce.6.cloned.1.call-start = ((), (), s32[]{:S(2)}) async-start(), calls=%async_computation.3 | async-start | bytes 17334272 | tf_op jit(solution)/shard_map/psum | solution.py:85
  129.4 3.9 copy-start.28
  133.4 1.2 copy-start.18
  134.9 1.6 copy-start.2
  138.4 1.0 copy-start.19
  139.4 3.1 copy-start.1
  139.4 3.1 copy-start.17
  272.8 2.7 copy-start.3
  275.5 6.6 %copy-start.29 = (f32[512,512]{1,0:T(8,128)S(1)}, f32[512,512]{1,0:T(8,128)}, u32[]{:S(2)}) copy-start(f32[512,512]{1,0:T(8,128)} %param.22) | copy-start | bytes 3145732
  282.1 3.7 copy-start.23
  282.1 2.6 copy-start.8
  285.8 2.8 copy-start.24
  288.5 4.6 copy-start.15
  293.1 1.5 copy-start.10
  294.6 1.0 copy-start.21
  307.0 3.8 copy-start.5
  310.8 1.3 copy-start.6
  310.8 2.3 copy-start.33
  313.2 7.9 %copy-start.31 = (f32[512,512]{1,0:T(8,128)S(1)}, f32[512,512]{1,0:T(8,128)}, u32[]{:S(2)}) copy-start(f32[512,512]{1,0:T(8,128)} %param.20) | copy-start | bytes 3145732
  313.2 15.2 %slice-start = ((s8[6291456]{0:T(1024)(128)(4,1)}), s8[4194304]{0:T(1024)(128)(4,1)S(1)}, s32[]{:S(2)}) async-start(s8[6291456]{0:T(1024)(128)(4,1)} %bitcast.30), calls=%async_computation.4 | async-start | bytes 8388608
  321.1 7.3 %slice-start.1 = ((s8[6291456]{0:T(1024)(128)(4,1)}), s8[2097152]{0:T(1024)(128)(4,1)S(1)}, s32[]{:S(2)}) async-start(s8[6291456]{0:T(1024)(128)(4,1)} %bitcast.30), calls=%async_computation.5 | async-start | bytes 4194304
  381.1 42.4 %all-to-all-start.1 = ((f32[128,8,512]{2,1,0:T(8,128)}), f32[128,8,512]{2,1,0:T(8,128)}, u32[]{:S(2)}, u32[]{:S(2)}) async-start(f32[128,8,512]{2,1,0:T(8,128)} %slice_bitcast_fusion), calls=%async_computation.1 | async-start | bytes 4194304 | tf_op jit(solution)/shard_map/all_to_all | solution.py:77
  558.5 6.3 %copy-start.7 = (f32[642,1024]{1,0:T(8,128)S(1)}, f32[642,1024]{1,0:T(8,128)}, u32[]{:S(2)}) copy-start(f32[642,1024]{1,0:T(8,128)} %constant_dynamic-update-slice_fusion.3) | copy-start | bytes 7888900
  558.5 6.3 %copy-start.16 = (f32[642,512]{1,0:T(8,128)S(1)}, f32[642,512]{1,0:T(8,128)}, u32[]{:S(2)}) copy-start(f32[642,512]{1,0:T(8,128)} %copy-done.15) | copy-start | bytes 3944452
  558.5 6.3 %copy-start.22 = (f32[1024,512]{1,0:T(8,128)S(1)}, f32[1024,512]{1,0:T(8,128)}, u32[]{:S(2)}) copy-start(f32[1024,512]{1,0:T(8,128)} %get-tuple-element.28) | copy-start | bytes 6291460
  564.8 6.8 %copy-start.9 = (f32[642,512]{1,0:T(8,128)S(1)}, f32[642,512]{1,0:T(8,128)}, u32[]{:S(2)}) copy-start(f32[642,512]{1,0:T(8,128)} %param.24) | copy-start | bytes 3944452
  564.8 6.7 %copy-start.11 = (f32[642,1024]{1,0:T(8,128)S(1)}, f32[642,1024]{1,0:T(8,128)}, u32[]{:S(2)}) copy-start(f32[642,1024]{1,0:T(8,128)} %copy-done.10) | copy-start | bytes 7888900
  564.8 6.7 %copy-start.25 = (f32[642,512]{1,0:T(8,128)S(1)}, f32[642,512]{1,0:T(8,128)}, u32[]{:S(2)}) copy-start(f32[642,512]{1,0:T(8,128)} %get-tuple-element.25) | copy-start | bytes 3944452
  571.6 1.5 copy-start.26
  571.6 2.9 copy-start.20
Sparse Core Ops, SparseCore 0:
  129.5 143.2 all-reduce.3
  378.0 180.4 all-reduce.5
where the time goes:
time: 594 us; the launch traced here: 584 us
  waiting for transfers between devices  283 us (48%)
  matrix products  98.8 us (17%)
  local copies, waits for them, and re-layouts  95.2 us (16%)
  other arithmetic  72.5 us (12%)
  starting transfers between devices  19.1 us (3%)
  between operations  14.7 us (2%)
    psum x1, waiting for transfers between devices, per_device(): coarse_agg = lax.psum(coarse_part, 'patch')  127 us
    psum x1, waiting for transfers between devices, per_device(): grad_coarse = grad_coarse_direct + lax.psum(coarse_grad_part, 'patch')  126 us
    dot_general x18, matrix products, mat_mul(): jnp.dot(left, right, precision=lax.Precision.HIGHEST, preferred_element_t...  98.8 us
    unnamed x80, local copies, waits for them, and re-layouts  27.9 us
    all_to_all x1, waiting for transfers between devices, per_device(): lax.all_to_all(grad_halo, 'patch', split_axis=0, concat_axis=0, tiled=True)  19.7 us
    scatter-add x1, other arithmetic, per_device(): jax.ops.segment_sum(new_edges, receivers, num_segments=near_rows)  19.4 us
    concatenate x1, local copies, waits for them, and re-layouts, per_device(): jnp.concatenate([near_table, incoming.reshape(-1, feat_dim)], axis=0)  12.5 us
    all_to_all x1, starting transfers between devices, per_device(): lax.all_to_all(outgoing, 'patch', split_axis=0, concat_axis=0, tiled=True)  12 us
  transfers between devices with their start and end apart: 4, of which 4 were waited for; matrix products, arithmetic and copies ran while one was open for 11% of the time, Pallas kernels for 0%

commit v1 on v0

v1 whole, which is shorter than its diff:
```python
import functools
import math

import jax
import jax.numpy as jnp
from jax import lax
from jax.experimental import pallas as pl
from jax.experimental.pallas import tpu as pltpu
from jax.sharding import PartitionSpec as P

MESH = pl.DeviceIdType.MESH
F32 = jnp.float32
BF16 = jnp.bfloat16
FEAT = 512
FINE = 256
COARSE = 642
NEAR = 1024
EDGE = 1024
BLOCK = 256
LINKS = 6
VMEM_BYTES = 60 << 20

NN = (((1,), (0,)), ((), ()))
NT = (((1,), (1,)), ((), ()))
TN = (((0,), (0,)), ((), ()))


def split(value):
    high = value.astype(BF16)
    return high, (value - high.astype(F32)).astype(BF16)


def dot(left, right, dims=NN):
    return lax.dot_general(left, right, dims, preferred_element_type=F32)


def dot3(left, right, dims=NN):
    return dot(left[0], right[0], dims) + dot(left[0], right[1], dims) + dot(left[1], right[0], dims)


def dot2(left, right, dims=NN):
    return dot(left, right[0], dims) + dot(left, right[1], dims)


def block_at(step):
    return pl.ds(pl.multiple_of(step * BLOCK, BLOCK), BLOCK)


def pair_at(refs, rows):
    return refs[0][rows, :], refs[1][rows, :]


def put_pair(refs, rows, value):
    high, low = split(value)
    refs[0][rows, :] = high
    refs[1][rows, :] = low


def spread(index_row):
    return jnp.transpose(jnp.broadcast_to(index_row, (128, index_row.shape[1])))


def hot_rows(spread_block, first, width):
    lane = lax.broadcasted_iota(jnp.int32, (spread_block.shape[0], 128), 1)
    local = spread_block - first
    tiles = [jnp.where(local == lane + at, 1.0, 0.0).astype(BF16) for at in range(0, width, 128)]
    return jnp.concatenate(tiles, axis=1)


def hot_columns(index_row, first, height):
    row = lax.broadcasted_iota(jnp.int32, (height, index_row.shape[1]), 0) + first
    return jnp.where(row == index_row, 1.0, 0.0).astype(BF16)


def sigmoid(value):
    return 1.0 / (1.0 + jnp.exp(-value))


def mean(value):
    return jnp.sum(value, axis=1, keepdims=True) * (1.0 / FEAT)


def norm(value):
    center = value - mean(value)
    scale = lax.rsqrt(mean(center * center) + 1e-05)
    return center * scale, scale


def norm_back(grad, normed, scale):
    return scale * (grad - mean(grad) - normed * mean(grad * normed))


def put_tiles(ref, value):
    for at in range(FEAT // 128):
        ref[:, at] = value[:, at * 128 : (at + 1) * 128].reshape(-1, 8, 128)


def vmem_specs(count):
    return [pl.BlockSpec(memory_space=pltpu.VMEM)] * count


def local_call(kernel, outs, scratch, flops, *args):
    moved = sum(math.prod(a.shape) * 4 for a in args) + sum(math.prod(o.shape) * 4 for o in outs)
    return pl.pallas_call(
        kernel,
        out_shape=outs,
        in_specs=vmem_specs(len(args)),
        out_specs=vmem_specs(len(outs)),
        scratch_shapes=scratch,
        compiler_params=pltpu.CompilerParams(vmem_limit_bytes=VMEM_BYTES),
        cost_estimate=pl.CostEstimate(flops=int(flops), bytes_accessed=moved, transcendentals=0),
    )(*args)


def f32_out(*shape):
    return jax.ShapeDtypeStruct(shape, F32)


def bf16_out(*shape):
    return jax.ShapeDtypeStruct(shape, BF16)


TILES = f32_out(64, 4, 8, 128)


def outgoing_kernel(fine_ref, w_ref, list_ref, out_ref, own_ref, list_rep):
    own = dot3(split(fine_ref[...]), split(w_ref[FEAT : 2 * FEAT, :]))
    own_ref[...] = own
    parts = split(own)
    list_rep[...] = spread(list_ref[...])

    def step(at, carry):
        rows = block_at(at)
        out_ref[rows, :] = dot2(hot_rows(list_rep[rows, :], 0, FINE), parts)
        return carry

    lax.fori_loop(0, EDGE // BLOCK, step, 0)


def near_kernel(near_ref, own_ref, edge_ref, w_ref, send_ref, recv_ref, pre_ref, p0, p1, q0, q1, send_rep, recv_rep):
    put_pair((p0, p1), pl.ds(0, FINE), own_ref[...])
    send_rep[...] = spread(send_ref[...])
    recv_rep[...] = spread(recv_ref[...])
    w_send = split(w_ref[FEAT : 2 * FEAT, :])
    w_recv = split(w_ref[2 * FEAT :, :])

    put_pair((q0, q1), pl.ds(0, FINE), dot3(split(near_ref[:FINE, :]), w_recv))

    def project(at, carry):
        rows = block_at(at)
        feats = split(near_ref[rows, :])
        put_pair((p0, p1), rows, dot3(feats, w_send))
        put_pair((q0, q1), rows, dot3(feats, w_recv))
        return carry

    lax.fori_loop(1, NEAR // BLOCK, project, 0)
    w_edge = split(w_ref[:FEAT, :])

    def step(at, carry):
        rows = block_at(at)
        total = dot3(split(edge_ref[rows, :]), w_edge)
        total += dot2(hot_rows(recv_rep[rows, :], 0, NEAR), (q0[...], q1[...]))
        total += dot2(hot_rows(send_rep[rows, :], 0, NEAR), (p0[...], p1[...]))
        pre_ref[rows, :] = total
        return carry

    lax.fori_loop(0, EDGE // BLOCK, step, 0)


def edge_kernel(part_ref, halo_ref, edge_ref, w_ref, send_ref, recv_ref, pre_ref, normed_ref, scale_ref, agg_ref, h0, h1, n0, n1, send_rep):
    send_rep[...] = spread(send_ref[...])
    h0[...], h1[...] = split(halo_ref[...])
    w_out = split(w_ref[...])

    def step(at, carry):
        rows = block_at(at)
        pre = part_ref[rows, :] + dot2(hot_rows(send_rep[rows, :], NEAR, EDGE), (h0[...], h1[...]))
        pre_ref[rows, :] = pre
        normed, scale = norm(dot3(split(pre * sigmoid(pre)), w_out))
        normed_ref[rows, :] = normed
        scale_ref[rows, :] = jnp.broadcast_to(scale, (BLOCK, 128))
        put_pair((n0, n1), rows, edge_ref[rows, :] + normed)
        return carry

    lax.fori_loop(0, EDGE // BLOCK, step, 0)

    def gather(at, carry):
        rows = block_at(at)
        agg_ref[rows, :] = dot2(hot_columns(recv_ref[...], at * BLOCK, BLOCK), (n0[...], n1[...]))
        return carry

    lax.fori_loop(0, NEAR // BLOCK, gather, 0)


def cube_place():
    me = lax.axis_index("patch")
    core = me % 2
    y = (me // 2) % 4
    x = (me // 8) % 4
    z = me // 32
    bits, mates = [core], [me + 1 - 2 * core]
    for low in (True, False):
        for place, stride in ((z, 32), (x, 8), (y, 2)):
            if low:
                bits.append(((place + 1) // 2) % 2)
                mates.append(me + (1 - 2 * (place % 2)) * stride)
            else:
                bits.append(place // 2)
                mates.append(me + (3 - 2 * place) * stride)
    return bits, mates


def greet(mates):
    barrier = pltpu.get_barrier_semaphore()
    for mate in mates:
        pl.semaphore_signal(barrier, inc=1, device_id=(mate,), device_id_type=MESH)
    pl.semaphore_wait(barrier, len(mates))


def push(src, dst, send_sem, recv_sem, mate):
    copy = pltpu.make_async_remote_copy(
        src_ref=src, dst_ref=dst, send_sem=send_sem, recv_sem=recv_sem, device_id=(mate,), device_id_type=MESH
    )
    copy.start()
    return copy


def cube_bit(part, step):
    return 0 if step == 0 else 1 + (part + step - 1) % LINKS


def sum_kernel(*refs):
    weight_refs, (coarse_ref, direct_ref), (out_ref,) = refs[:6], refs[6:8], refs[8:9]
    buf, got, s1, r1, s2, r2 = refs[9:]
    flat = buf.reshape(LINKS * 128 * 3, 8, 128)
    at = 0
    for ref in weight_refs:
        size = ref.shape[0] * 4
        flat[at : at + size] = ref[...].reshape(size, 8, 128)
        at += size
    size = coarse_ref.shape[0] * 4
    flat[at : at + size] = coarse_ref[...].reshape(size, 8, 128)
    flat[at + size :] = jnp.zeros((flat.shape[0] - at - size, 8, 128), F32)
    me = lax.axis_index("patch")
    mine = pl.ds(at + me * 4, 4)
    flat[mine] += direct_ref[...]
    bits, mates = cube_place()
    greet(mates)

    bases = [0] * LINKS
    copies = {}

    def reduce_start(part, step):
        bit = cube_bit(part, step)
        half = 64 >> step
        away = bases[part] + (1 - bits[bit]) * half
        copies[part] = push(
            buf.at[part, pl.ds(away, half)], got.at[part, pl.ds(128 - 2 * half, half)], s1.at[step, part], r1.at[step, part], mates[bit]
        )
        bases[part] = bases[part] + bits[bit] * half

    def gather_start(part, step):
        bit = cube_bit(part, step)
        half = 64 >> step
        block = out_ref.at[part, pl.ds(bases[part], half)]
        copies[part] = push(block, block, s2.at[step, part], r2.at[step, part], mates[bit])
        bases[part] = bases[part] - bits[bit] * half

    for part in range(LINKS):
        reduce_start(part, 0)
    for step in range(7):
        half = 64 >> step
        for part in range(LINKS):
            copies[part].wait()
            kept = pl.ds(bases[part], half)
            arrived = got[part, pl.ds(128 - 2 * half, half)]
            if step < 6:
                buf[part, kept] += arrived
                reduce_start(part, step + 1)
            else:
                out_ref[part, kept] = buf[part, kept] + arrived
                gather_start(part, step)
    for step in reversed(range(7)):
        for part in range(LINKS):
            copies[part].wait()
            if step > 0:
                gather_start(part, step - 1)


def sum_all(weights, coarse, direct):
    sem = pltpu.SemaphoreType.DMA((7, LINKS))
    shape = (LINKS, 128, 3, 8, 128)
    return pl.pallas_call(
        sum_kernel,
        out_shape=f32_out(*shape),
        in_specs=vmem_specs(8),
        out_specs=pl.BlockSpec(memory_space=pltpu.VMEM),
        scratch_shapes=[pltpu.VMEM(shape, F32), pltpu.VMEM((LINKS, 127, 3, 8, 128), F32)] + [sem] * 4,
        compiler_params=pltpu.CompilerParams(collective_id=1, has_side_effects=True, vmem_limit_bytes=VMEM_BYTES),
    )(*weights, coarse, direct)


COLUMN_ORDERS = ((0, 1, 2), (1, 2, 0), (2, 0, 1), (0, 2, 1))
STRIDES = (32, 8, 2)


def axis_places(device):
    return [(device // 32) % 4, (device // 8) % 4, (device // 2) % 4], device % 2


def position(device, part):
    places, core = axis_places(device)
    spot = core
    for axis in COLUMN_ORDERS[part]:
        spot = spot * 4 + places[axis]
    return spot


def node_pass(feats, agg, cot, w_in, w_out):
    feat_pair, agg_pair = split(feats), split(agg)
    pre = dot3(feat_pair, pair_at(w_in, pl.ds(0, FEAT))) + dot3(agg_pair, pair_at(w_in, pl.ds(FEAT, FEAT)))
    gate = sigmoid(pre)
    hidden = split(pre * gate)
    out_pair = (w_out[0][...], w_out[1][...])
    normed, scale = norm(dot3(hidden, out_pair))
    tail = split(norm_back(cot, normed, scale))
    grad_pre = split(dot3(tail, out_pair, NT) * (gate * (1.0 + pre * (1.0 - gate))))
    return feat_pair, agg_pair, hidden, tail, grad_pre


def node_kernel(*refs):
    agg_ref, fine_ref, cot_ref, few_ref, few_cot_ref, w_in_ref, w_out_ref = refs[:7]
    grad_agg_ref, own_ref, direct_ref, in_ref, out_ref = refs[7:12]
    buf, got, full, wi0, wi1, wo0, wo1, total = refs[12:20]
    s1, r1, s2, r2 = refs[20:]
    me = lax.axis_index("patch")
    places, core = axis_places(me)
    mate = me + 1 - 2 * core

    def peer(axis, shift):
        return me + ((places[axis] + shift) % 4 - places[axis]) * STRIDES[axis]

    for part in range(4):
        for device in range(128):
            first = FINE + 8 * device
            if first < NEAR and 8 * device < COARSE:
                buf[part, position(device, part)] = agg_ref[first : first + 8, part * 128 : (part + 1) * 128]
            else:
                buf[part, position(device, part)] = jnp.zeros((8, 128), F32)
    greet([mate] + [peer(axis, shift) for axis in range(3) for shift in (1, 2, 3)])

    wi, wo = (wi0, wi1), (wo0, wo1)
    keep = {}

    def cut_weights():
        wi0[...], wi1[...] = split(w_in_ref[...])
        wo0[...], wo1[...] = split(w_out_ref[...])

    def fine_pass():
        keep["fine"] = node_pass(fine_ref[...], agg_ref[:FINE, :], cot_ref[...], wi, wo)

    def fine_back():
        grad_pre = keep["fine"][4]
        own_ref[...] = cot_ref[...] + dot3(grad_pre, pair_at(wi, pl.ds(0, FEAT)), NT)
        grad_agg_ref[:FINE, :] = dot3(grad_pre, pair_at(wi, pl.ds(FEAT, FEAT)), NT)

    beside = [cut_weights, fine_pass, fine_back]

    bases = [0] * 4
    for stage in range(4):
        sub = (64, 16, 4, 1)[stage]
        offset = (0, 64, 112, 124)[stage]
        copies = []
        for part in range(4):
            if stage == 0:
                away = (1 - core) * sub
                copies.append(push(buf.at[part, pl.ds(away, sub)], got.at[part, pl.ds(0, sub)], s1.at[part, 0], r1.at[part, 0], mate))
                bases[part] = core * sub
                continue
            axis = COLUMN_ORDERS[part][stage - 1]
            for shift in (1, 2, 3):
                away = bases[part] + ((places[axis] + shift) % 4) * sub
                sem = 3 * stage - 3 + shift
                copies.append(
                    push(
                        buf.at[part, pl.ds(away, sub)],
                        got.at[part, pl.ds(offset + (shift - 1) * sub, sub)],
                        s1.at[part, sem],
                        r1.at[part, sem],
                        peer(axis, shift),
                    )
                )
            bases[part] = bases[part] + places[axis] * sub
        if beside:
            beside.pop(0)()
        count = len(copies) // 4
        for part in range(4):
            for copy in copies[part * count : (part + 1) * count]:
                copy.wait()
            kept = pl.ds(bases[part], sub)
            value = buf[part, kept]
            for shift in range(count):
                value += got[part, pl.ds(offset + shift * sub, sub)]
            buf[part, kept] = value

    few_agg = jnp.concatenate([buf[part, bases[part]] for part in range(4)], axis=1)
    blank = jnp.zeros((8, FEAT), F32)
    few = node_pass(
        jnp.concatenate([few_ref[...], blank], axis=0),
        jnp.concatenate([few_agg, blank], axis=0),
        jnp.concatenate([few_cot_ref[...], blank], axis=0),
        wi,
        wo,
    )
    few_grad = dot3(few[4], pair_at(wi, pl.ds(FEAT, FEAT)), NT)[:8]
    for part in range(4):
        full[part, bases[part]] = few_grad[:, part * 128 : (part + 1) * 128]

    def few_back():
        direct = few_cot_ref[...] + dot3(few[4], pair_at(wi, pl.ds(0, FEAT)), NT)[:8]
        for at in range(4):
            direct_ref[at] = direct[:, at * 128 : (at + 1) * 128]

    def weights_back(which, grad, ref, first):
        def run():
            total[...] = dot3(keep["fine"][which], keep["fine"][grad], TN) + dot3(few[which], few[grad], TN)
            put_tiles(ref.at[pl.ds(first, 64)], total)

        return run

    beside = [few_back, weights_back(0, 4, in_ref, 0), weights_back(1, 4, in_ref, 64), weights_back(2, 3, out_ref, 0)]
    for stage in (3, 2, 1, 0):
        sub = (64, 16, 4, 1)[stage]
        copies = []
        for part in range(4):
            block = full.at[part, pl.ds(bases[part], sub)]
            if stage == 0:
                copies.append(push(block, block, s2.at[part, 0], r2.at[part, 0], mate))
                continue
            axis = COLUMN_ORDERS[part][stage - 1]
            for shift in (1, 2, 3):
                sem = 3 * stage - 3 + shift
                copies.append(push(block, block, s2.at[part, sem], r2.at[part, sem], peer(axis, shift)))
            bases[part] = bases[part] - places[axis] * sub
        if beside:
            beside.pop(0)()
        for copy in copies:
            copy.wait()
    for part in range(4):
        for device in range((NEAR - FINE) // 8):
            first = FINE + 8 * device
            grad_agg_ref[first : first + 8, part * 128 : (part + 1) * 128] = full[part, position(device, part)]


def node_step(agg, fine, cot_fine, few, few_cot, w_in, w_out):
    sem = pltpu.SemaphoreType.DMA((4, 10))
    return pl.pallas_call(
        node_kernel,
        out_shape=[f32_out(NEAR, FEAT), f32_out(FINE, FEAT), f32_out(4, 8, 128), f32_out(128, 4, 8, 128), TILES],
        in_specs=vmem_specs(7),
        out_specs=vmem_specs(5),
        scratch_shapes=[
            pltpu.VMEM((4, 128, 8, 128), F32),
            pltpu.VMEM((4, 127, 8, 128), F32),
            pltpu.VMEM((4, 128, 8, 128), F32),
            pltpu.VMEM((2 * FEAT, FEAT), BF16),
            pltpu.VMEM((2 * FEAT, FEAT), BF16),
            pltpu.VMEM((FEAT, FEAT), BF16),
            pltpu.VMEM((FEAT, FEAT), BF16),
            pltpu.VMEM((FEAT, FEAT), F32),
        ]
        + [sem] * 4,
        compiler_params=pltpu.CompilerParams(collective_id=2, has_side_effects=True, vmem_limit_bytes=VMEM_BYTES),
    )(agg, fine, cot_fine, few, few_cot, w_in, w_out)


def edge_back_kernel(grad_agg_ref, cot_ref, pre_ref, normed_ref, scale_ref, w_ref, send_ref, recv_ref, grad_ref, t0, t1, d0, d1, halo_ref, a0, a1, recv_rep):
    recv_rep[...] = spread(recv_ref[...])
    a0[...], a1[...] = split(grad_agg_ref[...])
    w_out = split(w_ref[...])

    def step(at, carry):
        rows = block_at(at)
        grad = cot_ref[rows, :] + dot2(hot_rows(recv_rep[rows, :], 0, NEAR), (a0[...], a1[...]))
        grad_ref[rows, :] = grad
        tail = split(norm_back(grad, normed_ref[rows, :], scale_ref[rows, :1]))
        t0[rows, :], t1[rows, :] = tail
        pre = pre_ref[rows, :]
        gate = sigmoid(pre)
        put_pair((d0, d1), rows, dot3(tail, w_out, NT) * (gate * (1.0 + pre * (1.0 - gate))))
        return carry

    lax.fori_loop(0, EDGE // BLOCK, step, 0)

    def gather(at, carry):
        rows = block_at(at)
        halo_ref[rows, :] = dot2(hot_columns(send_ref[...], NEAR + at * BLOCK, BLOCK), (d0[...], d1[...]))
        return carry

    lax.fori_loop(0, EDGE // BLOCK, gather, 0)


def weights_kernel(*refs):
    grad_ref, t0, t1, d0, d1, pre_ref, edge_ref, near_ref, w_ref, send_ref, recv_ref = refs[:11]
    grad_edges_ref, in_edge_ref, in_send_ref, in_recv_ref, out_ref, own_send_ref, own_ref, coarse_ref = refs[11:19]
    edge_total, tail_total, recv_total = refs[19:]
    edge_total[...] = jnp.zeros_like(edge_total)
    tail_total[...] = jnp.zeros_like(tail_total)
    w_edge = split(w_ref[:FEAT, :])

    def step(at, carry):
        rows = block_at(at)
        grad_pre = (d0[rows, :], d1[rows, :])
        grad_edges_ref[rows, :] = grad_ref[rows, :] + dot3(grad_pre, w_edge, NT)
        edge_total[...] += dot3(split(edge_ref[rows, :]), grad_pre, TN)
        pre = pre_ref[rows, :]
        tail_total[...] += dot3(split(pre * sigmoid(pre)), (t0[rows, :], t1[rows, :]), TN)
        return carry

    lax.fori_loop(0, EDGE // BLOCK, step, 0)
    put_tiles(in_edge_ref, edge_total)
    put_tiles(out_ref, tail_total)
    w_send = split(w_ref[FEAT : 2 * FEAT, :])
    w_recv = split(w_ref[2 * FEAT :, :])

    def sums(at):
        grad_pre = (d0[...], d1[...])
        sent = dot2(hot_columns(send_ref[...], at * BLOCK, BLOCK), grad_pre)
        return sent, split(dot2(hot_columns(recv_ref[...], at * BLOCK, BLOCK), grad_pre))

    sent, received = sums(0)
    own_send_ref[...] = sent
    own_ref[...] = dot3(received, w_recv, NT)
    recv_total[...] = dot3(split(near_ref[:FINE, :]), received, TN)
    in_send_ref[...] = jnp.zeros_like(in_send_ref)

    def coarse_step(at, carry):
        rows = block_at(at)
        sent, received = sums(at)
        sent = split(sent)
        value = dot3(sent, w_send, NT) + dot3(received, w_recv, NT)
        put_tiles(coarse_ref.at[pl.ds((at - 1) * (BLOCK // 8), BLOCK // 8)], value)
        feats = split(near_ref[rows, :])
        recv_total[...] += dot3(feats, received, TN)
        in_send_ref[...] += dot3(feats, sent, TN)
        return carry

    lax.fori_loop(1, NEAR // BLOCK, coarse_step, 0)
    put_tiles(in_recv_ref, recv_total)


def fine_kernel(back_ref, list_ref, own_send_ref, own_ref, direct_ref, fine_ref, w_ref, partial_ref, grad_ref, in_send_ref):
    sent = split(own_send_ref[...] + dot2(hot_columns(list_ref[...], 0, FINE), split(back_ref[...])))
    grad_ref[...] = direct_ref[...] + own_ref[...] + dot3(sent, split(w_ref[FEAT : 2 * FEAT, :]), NT)
    put_tiles(in_send_ref, partial_ref[...] + dot3(split(fine_ref[...]), sent, TN))


def per_device(
    fine_nodes,
    coarse_nodes,
    edge_feats,
    senders,
    receivers,
    send_rows,
    w_edge_in,
    w_edge_out,
    w_node_in,
    w_node_out,
    cot_fine,
    cot_coarse,
    cot_edges,
):
    me = lax.axis_index("patch")
    peers = lax.axis_size("patch")
    send_list = send_rows.reshape(1, EDGE)
    near_count = FINE + COARSE
    send_at = jnp.where(senders < near_count, senders, senders + (NEAR - near_count)).reshape(1, EDGE)
    recv_at = receivers.reshape(1, EDGE)
    pair = [pltpu.VMEM((EDGE, FEAT), BF16)] * 2
    index = pltpu.VMEM((EDGE, 128), jnp.int32)
    square = pltpu.VMEM((FEAT, FEAT), F32)
    wide = f32_out(EDGE, FEAT)
    fine_out = f32_out(FINE, FEAT)

    outgoing, own = local_call(outgoing_kernel, [wide, fine_out], [index], 1e9, fine_nodes, w_edge_in, send_list)
    incoming = lax.all_to_all(outgoing.reshape(peers, 8, FEAT), "patch", split_axis=0, concat_axis=0, tiled=True)
    incoming = incoming.reshape(EDGE, FEAT)
    near = jnp.concatenate([fine_nodes, coarse_nodes, jnp.zeros((NEAR - near_count, FEAT), F32)], axis=0)
    pre_near = local_call(
        near_kernel, [wide], pair * 2 + [index] * 2, 1e10, near, own, edge_feats, w_edge_in, send_at, recv_at
    )[0]
    pre, normed, scale, agg = local_call(
        edge_kernel,
        [wide, wide, f32_out(EDGE, 128), wide],
        pair * 2 + [index],
        5e9,
        pre_near,
        incoming,
        edge_feats,
        w_edge_out,
        send_at,
        recv_at,
    )
    blank = jnp.zeros((8 * peers - COARSE, FEAT), F32)
    few = lax.dynamic_slice(jnp.concatenate([coarse_nodes, blank], axis=0), (me * 8, 0), (8, FEAT))
    few_cot = lax.dynamic_slice(jnp.concatenate([cot_coarse, blank], axis=0), (me * 8, 0), (8, FEAT))
    grad_agg, direct, few_direct, node_in, node_out = node_step(agg, fine_nodes, cot_fine, few, few_cot, w_node_in, w_node_out)
    half = bf16_out(EDGE, FEAT)
    grad, t0, t1, d0, d1, halo = local_call(
        edge_back_kernel,
        [wide, half, half, half, half, wide],
        pair + [index],
        8e9,
        grad_agg,
        cot_edges,
        pre,
        normed,
        scale,
        w_edge_out,
        send_at,
        recv_at,
    )
    back = lax.all_to_all(halo.reshape(peers, 8, FEAT), "patch", split_axis=0, concat_axis=0, tiled=True)
    grad_edges, in_edge, in_send, in_recv, edge_out, own_send, own_grad, coarse = local_call(
        weights_kernel,
        [wide, TILES, f32_out(FEAT, FEAT), TILES, TILES, fine_out, fine_out, f32_out(96, 4, 8, 128)],
        [square] * 3,
        1.6e10,
        grad,
        t0,
        t1,
        d0,
        d1,
        pre,
        edge_feats,
        near,
        w_edge_in,
        send_at,
        recv_at,
    )
    grad_fine, in_send = local_call(
        fine_kernel,
        [fine_out, TILES],
        [],
        2e9,
        back.reshape(EDGE, FEAT),
        send_list,
        own_send,
        own_grad,
        direct,
        fine_nodes,
        w_edge_in,
        in_send,
    )
    summed = sum_all((in_edge, in_send, in_recv, edge_out, node_in, node_out), coarse, few_direct)
    rows = summed.reshape(-1, 4, 8, 128).transpose(0, 2, 1, 3).reshape(-1, FEAT)
    edge_scale = 1.0 / math.sqrt(EDGE * peers)
    node_scale = 1.0 / math.sqrt(FINE * peers + COARSE)
    return (
        grad_fine,
        rows[7 * FEAT : 7 * FEAT + COARSE],
        grad_edges,
        rows[: 3 * FEAT] * edge_scale,
        rows[3 * FEAT : 4 * FEAT] * edge_scale,
        rows[4 * FEAT : 6 * FEAT] * node_scale,
        rows[6 * FEAT : 7 * FEAT] * node_scale,
    )


def solution(mesh):
    return jax.shard_map(
        per_device,
        mesh=mesh,
        in_specs=(
            P("patch", None),
            P(),
            P("patch", None),
            P("patch"),
            P("patch"),
            P("patch", None, None),
            P(),
            P(),
            P(),
            P(),
            P("patch", None),
            P(),
            P("patch", None),
        ),
        out_specs=(P("patch", None), P(), P("patch", None), P(), P(), P(), P()),
        check_vma=False,
    )
```

time: 594 us -> 265 us (0.45); the launches traced: 584 us -> 265 us
  waiting for transfers between devices: 283 us -> 18 us
  Pallas kernels: 0 us -> 210 us
  matrix products: 98.8 us -> 0 us
  local copies, waits for them, and re-layouts: 95.2 us -> 5.99 us
  other arithmetic: 72.5 us -> 12.3 us
  between operations: 14.7 us -> 0.71 us
    psum x2 -> x0, waiting for transfers between devices: 253 us -> none  [the longest x1 127 us: per_device(): coarse_agg = lax.psum(coarse_part, 'patch')]
    pallas_call x0 -> x8, Pallas kernels: none -> 210 us  [the longest x6 81.7 us: local_call(): pl.pallas_call(kernel, out_shape=outs, in_specs=vmem_specs(len(args)), ou...]
    dot_general x18 -> x0, matrix products: 98.8 us -> none  [mat_mul(): jnp.dot(left, right, precision=lax.Precision.HIGHEST, preferred_element_t...]
    scatter-add x4 -> x0, other arithmetic: 48.3 us -> none  [the longest x1 19.4 us: per_device(): jax.ops.segment_sum(new_edges, receivers, num_segments=near_rows)]
    gather x5 -> x0, local copies, waits for them, and re-layouts: 30.4 us -> none  [the longest x2 9.92 us: per_device(): grad_new_edges = cot_edges + grad_agg[receivers]]
    unnamed x80 -> x11, local copies, waits for them, and re-layouts: 27.9 us -> 2.13 us
    concatenate x3 -> x1, local copies, waits for them, and re-layouts: 16.7 us -> 0.07 us  [per_device(): jnp.concatenate([fine_nodes, coarse_nodes, jnp.zeros((NEAR - near_count,...]
    all_to_all x2, waiting for transfers between devices: 30.2 us -> 18 us  [the longest x1 12 us: per_device(): lax.all_to_all(outgoing.reshape(peers, 8, FEAT), 'patch', split_axis=0, c...]
  transfers between devices with their start and end apart: 4 -> 2, of which waited for: 4 -> 2; matrix products, arithmetic and copies ran while one was open for 11% -> 1% of each run, Pallas kernels for 0% -> 15%
where the time goes in v1:
time: 265 us
  Pallas kernels  210 us (79%)
  starting transfers between devices  18 us (7%)
  waiting for transfers between devices  18 us (7%)
  other arithmetic  12.3 us (5%)
  local copies, waits for them, and re-layouts  5.99 us (2%)
    pallas_call x6, Pallas kernels, local_call(): pl.pallas_call(kernel, out_shape=outs, in_specs=vmem_specs(len(args)), ou...  81.7 us
    pallas_call x1, Pallas kernels, sum_all(): pl.pallas_call(sum_kernel, out_shape=f32_out(*shape), in_specs=vmem_specs...  81 us
    pallas_call x1, Pallas kernels, node_step(): pl.pallas_call(node_kernel, out_shape=[f32_out(NEAR, FEAT), f32_out(FINE,...  47.4 us
    all_to_all x1, waiting for transfers between devices, per_device(): lax.all_to_all(outgoing.reshape(peers, 8, FEAT), 'patch', split_axis=0, c...  12 us
    all_to_all x1, starting transfers between devices, per_device(): lax.all_to_all(outgoing.reshape(peers, 8, FEAT), 'patch', split_axis=0, c...  12 us
    all_to_all x1, waiting for transfers between devices, per_device(): lax.all_to_all(halo.reshape(peers, 8, FEAT), 'patch', split_axis=0, conca...  6.02 us
    all_to_all x1, starting transfers between devices, per_device(): lax.all_to_all(halo.reshape(peers, 8, FEAT), 'patch', split_axis=0, conca...  6 us
  transfers between devices with their start and end apart: 2, of which 2 were waited for; matrix products, arithmetic and copies ran while one was open for 1% of the time, Pallas kernels for 15%

profile of v1, /device:TPU:1, one launch (start us, length us, event | category | flops | bytes accessed | tf_op | source)
XLA Modules:
  0.0 265.1 jit_solution(5652143705357586314)
XLA Ops:
  0.6 0.8 copy.21
  1.4 0.7 reshape.53.list_ref
  2.1 5.2 %shard_map.180 = (f32[1024,512]{1,0:T(8,128)}, f32[256,512]{1,0:T(8,128)}) custom-call(f32[256,512]{1,0:T(8,128)} %fine_ref.3, f32[1536,512]{1,0:T(8,128)} %w_ref.9, s32[1,1024]{1,0:T(1,128)} %reshape.53.list_ref), custom_call_target="tpu_custom_call" | custom-call | flops 1000000000 | bytes 6295552 | tf_op jit(solution)/shard_map/pallas_call | solution.py:104
  7.3 0.0 copy-start.1
  7.3 0.0 copy-start.3
  7.3 12.0 %all-to-all-start = ((f32[128,8,512]{2,1,0:T(8,128)}), f32[128,8,512]{2,1,0:T(8,128)}, u32[]{:S(2)}, u32[]{:S(2)}) async-start(f32[128,8,512]{2,1,0:T(8,128)} %bitcast.24), calls=%async_computation | async-start | bytes 4194304 | tf_op jit(solution)/shard_map/all_to_all | solution.py:586
  19.3 0.0 copy-start.4
  19.3 0.0 copy-start.2
  19.3 0.1 pad.4.clone
  19.4 0.0 copy-done.1
  19.4 0.0 copy-done.3
  19.4 0.6 pad_dynamic-slice_fusion
  20.0 0.0 copy-done.4
  20.0 0.6 compare_select_fusion
  20.6 0.0 copy-done.2
  20.6 1.5 maximum_maximum_fusion.near_ref.refs_7_
  22.1 15.3 %shard_map.181.part_ref = f32[1024,512]{1,0:T(8,128)} custom-call(f32[1024,512]{1,0:T(8,128)} %maximum_maximum_fusion.near_ref.refs_7_, f32[256,512]{1,0:T(8,128)} %get-tuple-element.34.own_ref, f32[1024,512]{1,0:T(8,128)} %refs_6_.3, f32[1536,512]{1,0:T(8,128)} %w_ref.9, s32[1,1024]{1,0:T(1,128)} %bitcast.26, s32[1,1024]{1,0:T(1,128)} %bitcast.30), custom_call_target="tpu_custom_call" | custom-call | flops 10000000000 | bytes 9969664 | tf_op jit(solution)/shard_map/pallas_call | solution.py:104
  37.4 12.0 %all-to-all-done = f32[128,8,512]{2,1,0:T(8,128)} async-done(((f32[128,8,512]{2,1,0:T(8,128)}), f32[128,8,512]{2,1,0:T(8,128)}, u32[]{:S(2)}, u32[]{:S(2)}) %all-to-all-start) | async-done | bytes 2097184 | tf_op jit(solution)/shard_map/all_to_all | solution.py:586
  49.4 14.8 %shard_map.182 = (f32[1024,512]{1,0:T(8,128)}, f32[1024,512]{1,0:T(8,128)}, f32[1024,128]{1,0:T(8,128)}, f32[1024,512]{1,0:T(8,128)}) custom-call(f32[1024,512]{1,0:T(8,128)} %shard_map.181.part_ref, f32[1024,512]{1,0:T(8,128)} %bitcast.3.halo_ref, f32[1024,512]{1,0:T(8,128)} %refs_6_.3, f32[512,512]{1,0:T(8,128)} %w_ref.8, s32[1,1024]{1,0:T(1,128)} %bitcast.27, ...), custom_call_target="tpu_custom_call" | custom-call | flops 5000000000 | bytes 14163968 | tf_op jit(solution)/shard_map/pallas_call | solution.py:104
  64.2 47.4 %shard_map.183 = (f32[1024,512]{1,0:T(8,128)}, f32[256,512]{1,0:T(8,128)}, f32[4,8,128]{2,1,0:T(8,128)}, f32[128,4,8,128]{3,2,1,0:T(8,128)}, f32[64,4,8,128]{3,2,1,0:T(8,128)}) custom-call(f32[1024,512]{1,0:T(8,128)} %get-tuple-element.36.refs_0_, f32[256,512]{1,0:T(8,128)} %fine_ref.3, f32[256,512]{1,0:T(8,128)} %refs_2_.1, ...), custom_call_target="tpu_custom_call" | custom-call | tf_op jit(solution)/shard_map/pallas_call | solution.py:457
  111.7 15.9 %shard_map.184 = (f32[1024,512]{1,0:T(8,128)}, bf16[1024,512]{1,0:T(8,128)(2,1)}, bf16[1024,512]{1,0:T(8,128)(2,1)}, bf16[1024,512]{1,0:T(8,128)(2,1)}, bf16[1024,512]{1,0:T(8,128)(2,1)}, /*index=5*/f32[1024,512]{1,0:T(8,128)}) custom-call(f32[1024,512]{1,0:T(8,128)} %get-tuple-element.37.grad_agg_ref, f32[1024,512]{1,0:T(8,128)} %cot_ref.1, ...), custom_call_target="tpu_custom_call" | custom-call | flops 8000000000 | bytes 22552576 | tf_op jit(solution)/shard_map/pallas_call | solution.py:104
  127.5 6.0 %all-to-all-start.1 = ((f32[128,8,512]{2,1,0:T(8,128)}), f32[128,8,512]{2,1,0:T(8,128)S(1)}, u32[]{:S(2)}, u32[]{:S(2)}) async-start(f32[128,8,512]{2,1,0:T(8,128)} %bitcast.25), calls=%async_computation.1 | async-start | bytes 4194304 | tf_op jit(solution)/shard_map/all_to_all | solution.py:623
  133.5 24.5 %shard_map.185 = (f32[1024,512]{1,0:T(8,128)}, f32[64,4,8,128]{3,2,1,0:T(8,128)}, f32[512,512]{1,0:T(8,128)}, f32[64,4,8,128]{3,2,1,0:T(8,128)}, f32[64,4,8,128]...) custom-call(f32[1024,512]{1,0:T(8,128)} %get-tuple-element.42.refs_0_, ...), custom_call_target="tpu_custom_call" | custom-call | flops 16000000000 | bytes 28844032 | tf_op jit(solution)/shard_map/pallas_call | solution.py:104
  158.0 6.0 %all-to-all-done.1 = f32[128,8,512]{2,1,0:T(8,128)S(1)} async-done(((f32[128,8,512]{2,1,0:T(8,128)}), f32[128,8,512]{2,1,0:T(8,128)S(1)}, u32[]{:S(2)}, u32[]{:S(2)}) %all-to-all-start.1) | async-done | bytes 2097184 | tf_op jit(solution)/shard_map/all_to_all | solution.py:623
  164.0 0.0 copy-start
  164.0 1.3 copy-done
  165.4 6.0 %shard_map.186 = (f32[256,512]{1,0:T(8,128)}, f32[64,4,8,128]{3,2,1,0:T(8,128)}) custom-call(f32[1024,512]{1,0:T(8,128)} %bitcast.23, s32[1,1024]{1,0:T(1,128)} %reshape.53.list_ref, f32[256,512]{1,0:T(8,128)} %get-tuple-element.47.own_send_ref, f32[256,512]{1,0:T(8,128)} %get-tuple-element.48.own_ref, f32[256,512]{1,0:T(8,128)} %get-tuple-element.49.direct_ref, ...), custom_call_target="tpu_custom_call" | custom-call | flops 2000000000 | bytes 9965568 | tf_op jit(solution)/shard_map/pallas_call | solution.py:104
  171.4 81.0 %shard_map.187 = f32[6,128,3,8,128]{4,3,2,1,0:T(8,128)} custom-call(f32[64,4,8,128]{3,2,1,0:T(8,128)} %get-tuple-element.52.refs_0_, f32[64,4,8,128]{3,2,1,0:T(8,128)} %get-tuple-element.53.refs_1_, f32[64,4,8,128]{3,2,1,0:T(8,128)} %get-tuple-element.54.refs_2_, f32[64,4,8,128]{3,2,1,0:T(8,128)} %get-tuple-element.55.refs_3_, ...), custom_call_target="tpu_custom_call" | custom-call | tf_op jit(solution)/shard_map/pallas_call | solution.py:293
  252.4 3.2 %fusion.1 = f32[1024,512]{1,0:T(8,128)} fusion(f32[576,8,4,128]{3,1,2,0:T(8,128)} %bitcast.19), kind=kLoop, calls=%fused_computation.3 | loop fusion | flops 524288 | bytes 4194304 | tf_op jit(solution)/shard_map/mul | solution.py:665
  255.6 3.1 %fusion.2 = (f32[512,512]{1,0:T(8,128)}, f32[512,512]{1,0:T(8,128)}) fusion(f32[576,8,4,128]{3,1,2,0:T(8,128)} %bitcast.20), kind=kLoop, calls=%fused_computation.8 | loop fusion | flops 524288 | bytes 4194304 | tf_op jit(solution)/shard_map/mul | solution.py:666
  258.7 3.9 %fusion = f32[1536,512]{1,0:T(8,128)} fusion(f32[576,8,4,128]{3,1,2,0:T(8,128)} %bitcast.21), kind=kLoop, calls=%fused_computation.1 | loop fusion | flops 786432 | bytes 6291456 | tf_op jit(solution)/shard_map/mul | solution.py:663
  262.6 2.5 slice.24
  (1 shorter events, 0.0 us)
Async XLA Ops:
  7.3 12.1 %copy-start.1 = (f32[642,512]{1,0:T(8,128)S(1)}, f32[642,512]{1,0:T(8,128)}, u32[]{:S(2)}) copy-start(f32[642,512]{1,0:T(8,128)} %param.14) | copy-start | bytes 3944452
  7.3 12.1 %copy-start.3 = (f32[642,512]{1,0:T(8,128)S(1)}, f32[642,512]{1,0:T(8,128)}, u32[]{:S(2)}) copy-start(f32[642,512]{1,0:T(8,128)} %param.24) | copy-start | bytes 3944452
  7.3 42.1 %all-to-all-start = ((f32[128,8,512]{2,1,0:T(8,128)}), f32[128,8,512]{2,1,0:T(8,128)}, u32[]{:S(2)}, u32[]{:S(2)}) async-start(f32[128,8,512]{2,1,0:T(8,128)} %bitcast.24), calls=%async_computation | async-start | bytes 4194304 | tf_op jit(solution)/shard_map/all_to_all | solution.py:586
  19.3 0.7 copy-start.4
  19.3 1.3 copy-start.2
  127.5 36.5 %all-to-all-start.1 = ((f32[128,8,512]{2,1,0:T(8,128)}), f32[128,8,512]{2,1,0:T(8,128)S(1)}, u32[]{:S(2)}, u32[]{:S(2)}) async-start(f32[128,8,512]{2,1,0:T(8,128)} %bitcast.25), calls=%async_computation.1 | async-start | bytes 4194304 | tf_op jit(solution)/shard_map/all_to_all | solution.py:623
  164.0 1.3 copy-start
